TPU v7x, 512 devices: a whole 4x4x16 slice. The times are simulated.
512 devices in a mesh: dp: 16 (over y, x), expert: 32 (over z, core).
Axes of the slice: x: 4, y: 4, z: 16, core: 2. Of those that a mesh axis runs over, the one named last changes fastest.
Arguments:
- inputs: bfloat16 [2048, 6144], P('expert', 'dp'), may hold values from -6 to 6
- grad_out: bfloat16 [2048, 6144], P('expert', 'dp'), may hold values from -6 to 6
- expert_ids: int32 [2048, 2], P('expert'), may hold values from 0 to 3, as said below
- live_counts: int32 [32], P('expert'), may hold values from 32 to 64, as said below
- router_weight: bfloat16 [6144, 4], P('dp'), may hold values from -0.078125 to 0.078125
- up_weight: bfloat16 [6144, 32768], P('dp', 'expert'), may hold values from -0.078125 to 0.078125
- down_weight: bfloat16 [6144, 32768], P('dp', 'expert'), may hold values from -0.0625 to 0.0625
Outputs:
- grad_inputs: bfloat16 [2048, 6144], P('expert', 'dp')
- grad_up: bfloat16 [6144, 32768], P('dp', 'expert')
- grad_down: bfloat16 [6144, 32768], P('dp', 'expert')
- grad_router: float32 [6144, 4], P('dp')
Inputs may be any that keep to these rules, and one draw needn't show every extreme that they name: `expert_ids`: each row names two different experts. Among the first live_counts[g] tokens of group g, each expert is named at most 32 times; one expert is named exactly 32 times in every group. `live_counts`: some group has all its slots live.
All inputs are finite; a program needn't handle non-finite values.
Results may differ from a plain program's by a relative error of at most 0.035.
Values may be sent and summed in bfloat16 or wider, within the bound.
A program may use at most 64 MiB of HBM per device.

v0:
```python
import jax
import jax.numpy as jnp
from jax import lax
from jax.sharding import PartitionSpec as P

ROOT_HALF = 0.7071067811865476
INV_ROOT_TWO_PI = 0.3989422804014327


def gelu_value(value):
    return 0.5 * value * (1.0 + jax.scipy.special.erf(value * ROOT_HALF))


def gelu_slope(value):
    return (
        0.5 * (1.0 + jax.scipy.special.erf(value * ROOT_HALF))
        + value * jnp.exp(-0.5 * value * value) * INV_ROOT_TWO_PI
    )


def activate(before_act, back_act, gate_column):
    active = gelu_value(before_act)
    hidden = lax.optimization_barrier(active.astype(jnp.bfloat16))
    gate_sum = jnp.sum(hidden.astype(jnp.float32) * back_act, axis=1)
    inner_grad = (gate_column * back_act * gelu_slope(before_act)).astype(jnp.bfloat16)
    weighted = (gate_column * active).astype(jnp.bfloat16)
    return (gate_sum, inner_grad, weighted)


def local(inputs, grad_out, expert_ids, live_counts, router_weight, up_weight, down_weight):
    per_group = inputs.shape[0]
    share = inputs.shape[1]
    experts = router_weight.shape[1]
    groups = lax.axis_size("expert")
    column_parts = groups // experts
    capacity = 2 * per_group // experts
    partial_logits = jnp.dot(inputs, router_weight, preferred_element_type=jnp.float32)
    logits = lax.psum(partial_logits, "dp")
    labels = jnp.arange(experts, dtype=jnp.int32)
    first_hot = (expert_ids[:, 0:1] == labels[None, :]).astype(jnp.float32)
    second_hot = (expert_ids[:, 1:2] == labels[None, :]).astype(jnp.float32)
    logit_gap = jnp.sum(logits * (first_hot - second_hot), axis=1)
    pick_gates = jnp.concatenate([jax.nn.sigmoid(logit_gap), jax.nn.sigmoid(-logit_gap)]).astype(
        jnp.bfloat16
    )
    pick_ids = jnp.concatenate([expert_ids[:, 0], expert_ids[:, 1]])
    position = jnp.arange(2 * per_group, dtype=jnp.int32) % per_group
    is_live = position < live_counts[0]
    one_hot = ((pick_ids[:, None] == labels[None, :]) & is_live[:, None]).astype(jnp.int32)
    pick_rank = jnp.sum(jnp.cumsum(one_hot, axis=0) * one_hot, axis=1) - 1
    overflow = experts * capacity
    pick_slot = jnp.where(is_live, pick_ids * capacity + pick_rank, overflow)
    slot_pick = (
        jnp.full((overflow,), 2 * per_group, jnp.int32)
        .at[pick_slot]
        .set(jnp.arange(2 * per_group, dtype=jnp.int32), mode="drop")
    )
    target = jnp.arange(groups * capacity, dtype=jnp.int32)
    expert_slot = target // capacity // column_parts * capacity + target % capacity
    send_pick = jnp.take(slot_pick, expert_slot, axis=0)
    send_token = jnp.where(send_pick < 2 * per_group, send_pick % per_group, per_group)
    send_rows = jnp.take(inputs, send_token, axis=0, mode="fill", fill_value=0)
    send_grad = jnp.take(grad_out, send_token, axis=0, mode="fill", fill_value=0)
    send_gate = jnp.take(pick_gates, send_pick, axis=0, mode="fill", fill_value=0)
    rows_in, rows_grad, gate_in = (
        lax.all_to_all(send_rows, "expert", split_axis=0, concat_axis=0, tiled=True),
        lax.all_to_all(send_grad, "expert", split_axis=0, concat_axis=0, tiled=True),
        lax.all_to_all(send_gate, "expert", split_axis=0, concat_axis=0, tiled=True),
    )
    before_part = jnp.dot(rows_in, up_weight, preferred_element_type=jnp.float32)
    back_part = jnp.dot(rows_grad, down_weight, preferred_element_type=jnp.float32)
    gate_column = gate_in.astype(jnp.float32)[:, None]
    before_act, back_act = (
        lax.psum(before_part.astype(jnp.bfloat16), "dp").astype(jnp.float32),
        lax.psum(back_part.astype(jnp.bfloat16), "dp").astype(jnp.float32),
    )
    gate_part, inner_grad, weighted = activate(before_act, back_act, gate_column)
    contract_rows = (((0,), (0,)), ((), ()))
    grad_up = lax.dot_general(
        rows_in, inner_grad, contract_rows, preferred_element_type=jnp.float32
    ).astype(jnp.bfloat16)
    grad_down = lax.dot_general(
        rows_grad, weighted, contract_rows, preferred_element_type=jnp.float32
    ).astype(jnp.bfloat16)
    contract_units = (((1,), (1,)), ((), ()))
    input_part = lax.dot_general(
        inner_grad, up_weight, contract_units, preferred_element_type=jnp.float32
    ).astype(jnp.bfloat16)
    back_rows, back_gate = (
        lax.all_to_all(input_part, "expert", split_axis=0, concat_axis=0, tiled=True),
        lax.all_to_all(
            gate_part.astype(jnp.bfloat16), "expert", split_axis=0, concat_axis=0, tiled=True
        ),
    )
    summed_rows = jnp.sum(
        back_rows.astype(jnp.float32).reshape(experts, column_parts, capacity, share), axis=1
    ).reshape(overflow, share)
    summed_gate = jnp.sum(
        back_gate.astype(jnp.float32).reshape(experts, column_parts, capacity), axis=1
    ).reshape(overflow)
    part_pick = jnp.take(summed_rows, pick_slot, axis=0, mode="fill", fill_value=0)
    gate_pick = jnp.take(summed_gate, pick_slot, axis=0, mode="fill", fill_value=0)
    gate_value = pick_gates.astype(jnp.float32)
    delta = lax.optimization_barrier(
        (gate_pick * gate_value * (1.0 - gate_value)).astype(jnp.bfloat16)
    ).astype(jnp.float32)
    delta_diff = delta[:per_group] - delta[per_group:]
    logit_grad = delta_diff[:, None] * (first_hot - second_hot)
    router_side = jnp.dot(
        logit_grad, router_weight.astype(jnp.float32).T, precision=lax.Precision.HIGHEST
    )
    grad_inputs = (
        grad_out.astype(jnp.float32) + (part_pick[:per_group] + part_pick[per_group:]) + router_side
    ).astype(jnp.bfloat16)
    router_term = jnp.dot(inputs.astype(jnp.float32).T, logit_grad, precision=lax.Precision.HIGHEST)
    grad_router = lax.psum(router_term, "expert")
    return (grad_inputs, grad_up, grad_down, grad_router)


def solution(mesh):
    placed = (
        P("expert", "dp"),
        P("expert", "dp"),
        P("expert", None),
        P("expert"),
        P("dp", None),
        P("dp", "expert"),
        P("dp", "expert"),
    )
    return jax.shard_map(
        local,
        mesh=mesh,
        in_specs=placed,
        out_specs=(P("expert", "dp"), P("dp", "expert"), P("dp", "expert"), P("dp", None)),
        check_vma=False,
    )
```

profile of v0, /device:TPU:1, one launch (start us, length us, event | category | flops | bytes accessed | tf_op | source)
XLA Modules:
  0.0 425.7 jit_solution(18165804764282503032)
XLA Ops:
  7.2 0.0 copy-start
  7.2 0.8 slice_bitcast_fusion.1
  8.6 0.1 pad_add_fusion
  8.7 0.1 fusion.17
  8.8 0.2 reduce_window_sum.11
  9.0 0.2 select_reduce_fusion
  9.2 0.1 fusion.52
  9.3 1.0 scatter_custom_fusion
  10.3 6.6 %gather_fusion = s32[1024]{0:T(1024)S(1)} fusion(s32[128]{0:T(128)S(1)} %scatter_custom_fusion, s32[1024]{0:T(1024)S(1)} %broadcast_clamp_fusion.2), kind=kCustom, calls=%fused_computation.2 | custom fusion | bytes 12288 | tf_op jit(solution)/shard_map/jit(_take)/gather | solution.py:60
  16.9 3.9 gather_fusion.4
  20.8 3.9 gather_fusion.5
  24.8 1.2 broadcast_select_fusion
  25.9 61.2 %all_to_all.45 = bf16[32,32,384]{2,1,0:T(8,128)(2,1)S(1)} all-to-all(bf16[32,32,384]{2,1,0:T(8,128)(2,1)S(1)} %bitcast.49), channel_id=1, replica_groups=mesh['dp'=16,'expert'=32] {'expert'}, dimensions={0} | all-to-all | bytes 1572864 | tf_op jit(solution)/shard_map/all_to_all | solution.py:66
  87.1 4.1 all-to-all-start.1
  91.2 0.0 all-reduce.3.cloned.1.call-start
  91.3 2.5 convolution_convert_fusion
  93.8 42.0 %all-to-all-done.1 = bf16[32,32,384]{2,1,0:T(8,128)(2,1)S(1)} async-done(((bf16[32,32,384]{2,1,0:T(8,128)(2,1)}), bf16[32,32,384]{2,1,0:T(8,128)(2,1)S(1)}, u32[]{:S(2)}, u32[]{:S(2)}) %all-to-all-start.1) | async-done | bytes 786464 | tf_op jit(solution)/shard_map/all_to_all | solution.py:67
  135.8 4.0 convolution_convert_fusion.1
  139.8 0.0 all-reduce.3.cloned.1.call-update
  139.9 0.1 fusion.58
  140.0 34.2 %psum.28 = f32[64,4]{0,1:T(4,128)S(1)} all-reduce(f32[64,4]{0,1:T(4,128)S(1)} %fusion.58), channel_id=1, replica_groups=mesh['dp'=16,'expert'=32] {'dp'}, use_global_device_ids=true, to_apply=%region_3.4 | all-reduce | flops 256 | bytes 2048 | tf_op jit(solution)/shard_map/psum | solution.py:38
  174.3 91.7 %all-reduce.3.cloned.1.call-done = (bf16[1024,1024]{1,0:T(8,128)(2,1)}, bf16[1024,1024]{1,0:T(8,128)(2,1)}) async-done(((bf16[1024,1024]{1,0:T(8,128)(2,1)}, bf16[1024,1024]{1,0:T(8,128)(2,1)}), (bf16[1024,1024]{1,0:T(8,128)(2,1)}, bf16[1024,1024]{1,0:T(8,128)(2,1)})) %all-reduce.3.cloned.1.call-update) | async-done | bytes 4194320 | tf_op jit(solution)/shard_map/psum | solution.py:75
  265.9 3.8 fusion.9
  269.7 0.6 fusion.2
  270.3 0.7 convert_element_type.131
  271.0 13.2 %all-to-all-start.4 = ((bf16[32,32,1]{1,2,0:T(2,128)(2,1)}), bf16[32,32,1]{1,2,0:T(2,128)(2,1)S(1)}, u32[]{:S(2)}, u32[]{:S(2)}) async-start(bf16[32,32,1]{1,2,0:T(2,128)(2,1)} %convert_element_type.131), calls=%async_computation.4 | async-start | bytes 32768 | tf_op jit(solution)/shard_map/all_to_all | solution.py:91
  284.2 0.1 gather.26
  284.3 11.6 %all-to-all-done.4 = bf16[32,32,1]{1,2,0:T(2,128)(2,1)S(1)} async-done(((bf16[32,32,1]{1,2,0:T(2,128)(2,1)}), bf16[32,32,1]{1,2,0:T(2,128)(2,1)S(1)}, u32[]{:S(2)}, u32[]{:S(2)}) %all-to-all-start.4) | async-done | bytes 2080 | tf_op jit(solution)/shard_map/all_to_all | solution.py:91
  296.0 0.1 reshape.485
  296.0 1.2 gather_fusion.3
  297.3 0.1 multiply_convert_fusion.4
  297.4 6.5 %gather_fusion.1 = bf16[1024]{0:T(1024)(128)(2,1)S(1)} fusion(bf16[128]{0:T(256)(128)(2,1)S(1)} %get-tuple-element.9, s32[1024]{0:T(1024)S(1)} %broadcast_clamp_fusion.1), kind=kCustom, calls=%fused_computation.3 | custom fusion | bytes 8192 | tf_op jit(solution)/shard_map/jit(_take)/gather | solution.py:64
  303.9 0.1 gather.29
  304.0 15.4 %all_to_all.46 = bf16[32,32,1]{1,2,0:T(2,128)(2,1)S(1)} all-to-all(bf16[32,32,1]{1,2,0:T(2,128)(2,1)S(1)} %copy.11), channel_id=1, replica_groups=mesh['dp'=16,'expert'=32] {'expert'}, dimensions={0} | all-to-all | bytes 4096 | tf_op jit(solution)/shard_map/all_to_all | solution.py:68
  319.4 0.1 convert_reduce_fusion.2
  319.5 0.1 reshape.486
  319.6 4.1 fusion.1
  323.7 2.2 convolution_convert_fusion.3
  325.8 5.1 %all-to-all-start.3 = ((bf16[32,32,384]{2,1,0:T(8,128)(2,1)}), bf16[32,32,384]{2,1,0:T(8,128)(2,1)}, u32[]{:S(2)}, u32[]{:S(2)}) async-start(bf16[32,32,384]{2,1,0:T(8,128)(2,1)} %bitcast.50), calls=%async_computation.3 | async-start | bytes 1572864 | tf_op jit(solution)/shard_map/all_to_all | solution.py:90
  330.9 0.1 slice_subtract_fusion
  331.0 0.1 convolution_bitcast_fusion
  331.1 76.7 %psum.31 = f32[384,4]{0,1:T(4,128)} all-reduce(f32[384,4]{0,1:T(4,128)S(1)} %convolution_bitcast_fusion), channel_id=1, replica_groups=mesh['dp'=16,'expert'=32] {'expert'}, use_global_device_ids=true, to_apply=%region_10.12 | all-reduce | flops 1536 | bytes 12288 | tf_op jit(solution)/shard_map/psum | solution.py:116
  407.9 3.8 convolution_convert_fusion.2
  411.7 4.2 fusion.13
  415.8 1.3 convert_reduce_fusion
  417.1 0.8 gather_fusion.2
  417.9 0.1 broadcast_select_fusion.2
  418.0 0.9 fusion.14
  (35 shorter events, 0.3 us)
Async XLA Ops:
  7.2 84.1 %copy-start = (bf16[384,1024]{1,0:T(8,128)(2,1)S(1)}, bf16[384,1024]{1,0:T(8,128)(2,1)}, u32[]{:S(2)}) copy-start(bf16[384,1024]{1,0:T(8,128)(2,1)} %param.14) | copy-start | bytes 2359300
  7.2 9.7 %copy-start.2 = (bf16[64,384]{1,0:T(8,128)(2,1)S(1)}, bf16[64,384]{1,0:T(8,128)(2,1)}, u32[]{:S(2)}) copy-start(bf16[64,384]{1,0:T(8,128)(2,1)} %param.10) | copy-start | bytes 147460
  16.8 4.0 copy-start.1
  87.1 52.7 %copy-start.6 = (bf16[32,32,384]{2,1,0:T(8,128)(2,1)}, bf16[32,32,384]{2,1,0:T(8,128)(2,1)S(1)}, u32[]{:S(2)}) copy-start(bf16[32,32,384]{2,1,0:T(8,128)(2,1)S(1)} %all_to_all.45) | copy-start | bytes 2359300
  87.1 48.7 %all-to-all-start.1 = ((bf16[32,32,384]{2,1,0:T(8,128)(2,1)}), bf16[32,32,384]{2,1,0:T(8,128)(2,1)S(1)}, u32[]{:S(2)}, u32[]{:S(2)}) async-start(bf16[32,32,384]{2,1,0:T(8,128)(2,1)} %bitcast.8), calls=%async_computation.1 | async-start | bytes 1572864 | tf_op jit(solution)/shard_map/all_to_all | solution.py:67
  91.2 174.7 %all-reduce.3.cloned.1.call-start = ((), (), s32[]{:S(2)}) async-start(), calls=%async_computation.5 | async-start | bytes 8388608 | tf_op jit(solution)/shard_map/psum | solution.py:75
  93.8 46.1 %copy-start.9 = (bf16[384,4]{0,1:T(4,128)(2,1)S(1)}, bf16[384,4]{0,1:T(4,128)(2,1)}, u32[]{:S(2)}) copy-start(bf16[384,4]{0,1:T(4,128)(2,1)} %param.13) | copy-start | bytes 9220
  135.8 130.1 %copy-start.7 = (bf16[32,32,384]{2,1,0:T(8,128)(2,1)}, bf16[32,32,384]{2,1,0:T(8,128)(2,1)S(1)}, u32[]{:S(2)}) copy-start(bf16[32,32,384]{2,1,0:T(8,128)(2,1)S(1)} %all-to-all-done.1) | copy-start | bytes 2359300
  265.9 3.8 copy-start.5
  269.7 49.8 %copy-start.3 = (bf16[1024,1024]{1,0:T(8,128)(2,1)S(1)}, bf16[1024,1024]{1,0:T(8,128)(2,1)}, u32[]{:S(2)}) copy-start(bf16[1024,1024]{1,0:T(8,128)(2,1)} %get-tuple-element.6) | copy-start | bytes 6291460
  271.0 24.9 %all-to-all-start.4 = ((bf16[32,32,1]{1,2,0:T(2,128)(2,1)}), bf16[32,32,1]{1,2,0:T(2,128)(2,1)S(1)}, u32[]{:S(2)}, u32[]{:S(2)}) async-start(bf16[32,32,1]{1,2,0:T(2,128)(2,1)} %convert_element_type.131), calls=%async_computation.4 | async-start | bytes 32768 | tf_op jit(solution)/shard_map/all_to_all | solution.py:91
  323.7 2.2 copy-start.4
  325.8 90.0 %all-to-all-start.3 = ((bf16[32,32,384]{2,1,0:T(8,128)(2,1)}), bf16[32,32,384]{2,1,0:T(8,128)(2,1)}, u32[]{:S(2)}, u32[]{:S(2)}) async-start(bf16[32,32,384]{2,1,0:T(8,128)(2,1)} %bitcast.50), calls=%async_computation.3 | async-start | bytes 1572864 | tf_op jit(solution)/shard_map/all_to_all | solution.py:90
  407.9 3.8 copy-start.8
Sparse Core Ops, SparseCore 0:
  140.0 125.8 all-reduce.2
where the time goes:
time: 426 us
  blocking collectives  188 us (44%)
  waiting for transfers between devices  145 us (34%)
  local copies, waits for them, and re-layouts  25.7 us (6%)
  starting transfers between devices  22.4 us (5%)
  matrix products  17.8 us (4%)
  between operations  14.9 us (3%)
  other arithmetic  12 us (3%)
    psum x1, waiting for transfers between devices, local(): lax.psum(back_part.astype(jnp.bfloat16), 'dp').astype(jnp.float32)  91.7 us
    psum x1, blocking collectives, local(): grad_router = lax.psum(router_term, 'expert')  76.7 us
    all_to_all x1, blocking collectives, local(): lax.all_to_all(send_rows, 'expert', split_axis=0, concat_axis=0, tiled=True)  61.2 us
    all_to_all x1, waiting for transfers between devices, local(): lax.all_to_all(send_grad, 'expert', split_axis=0, concat_axis=0, tiled=True)  42 us
    psum x1, blocking collectives, local(): logits = lax.psum(partial_logits, 'dp')  34.2 us
    all_to_all x1, blocking collectives, local(): lax.all_to_all(send_gate, 'expert', split_axis=0, concat_axis=0, tiled=True)  15.4 us
    all_to_all x1, starting transfers between devices, local(): lax.all_to_all(gate_part.astype(jnp.bfloat16), 'expert', split_axis=0, co...  13.2 us
    all_to_all x1, waiting for transfers between devices, local(): lax.all_to_all(gate_part.astype(jnp.bfloat16), 'expert', split_axis=0, co...  11.6 us
  transfers between devices with their start and end apart: 4, of which 3 were waited for; matrix products, arithmetic and copies ran while one was open for 3% of the time, Pallas kernels for 0%

commit v1 on v0

v1 whole, which is shorter than its diff:
```python
import jax
import jax.numpy as jnp
from jax import lax
from jax.experimental import pallas as pl
from jax.experimental.pallas import tpu as pltpu
from jax.sharding import PartitionSpec as P

MESH = pl.DeviceIdType.MESH
F32 = jnp.float32
BF16 = jnp.bfloat16
ROOT_HALF = 0.7071067811865476
INV_ROOT_TWO_PI = 0.3989422804014327

ORDERS = ((0, 2, 1, 3), (2, 1, 3, 0), (1, 3, 0, 2), (3, 0, 2, 1))
STEPS = 8
TICKS = 15
ROWS = 144
PARTS = ((0, 80), (80, 64))


def split(value):
    high = value.astype(BF16)
    return high, (value - high.astype(F32)).astype(BF16)


def dot(a, b, contract):
    return lax.dot_general(a, b, ((contract[:1], contract[1:]), ((), ())), preferred_element_type=F32)


def dot2(a, b, contract):
    high, low = split(a)
    return dot(high, b, contract) + dot(low, b, contract)


def route(a_row, b_row, expert):
    hit = jnp.where((a_row == expert) | (b_row == expert), 1.0, 0.0)
    upper = lax.broadcasted_iota(jnp.int32, (64, 64), 0) < lax.broadcasted_iota(jnp.int32, (64, 64), 1)
    rank = dot(
        jnp.broadcast_to(hit, (16, 64)).astype(BF16), jnp.where(upper, 1.0, 0.0).astype(BF16), (1, 0)
    )[0:1]
    slot = lax.broadcasted_iota(jnp.int32, (32, 64), 0).astype(F32)
    return jnp.where(slot == jnp.broadcast_to(rank, (32, 64)), jnp.broadcast_to(hit, (32, 64)), 0.0)


def signed_hot(a_row, b_row):
    row = lax.broadcasted_iota(jnp.int32, (16, 64), 0).astype(F32)
    first = jnp.where(row == jnp.broadcast_to(a_row, (16, 64)), 1.0, 0.0)
    second = jnp.where(row == jnp.broadcast_to(b_row, (16, 64)), 1.0, 0.0)
    return first - second


def kernel(
    x_ref, d_ref, meta_ref, rwt_ref, up_ref, down_ref,
    gi_ref, gu_ref, gd_ref, gr_ref,
    tb, pb, ph, ax, ad, part, rs0, rs1, rs2, ag, inn, wgt, pi, sx, rb, ret,
    ls, lr, gap, gaps, gp, gpr, gs, gret, dd, ddr,
    z_s, z_r, b_s, b_r, rs_s, rs_r, ag_s, ag_r, sx_s, sx_r, ret_s, ret_r,
    l_s, l_r, gap_s, gap_r, gp_s, gp_r, gr_s, gr_r, dd_s, dd_r,
):
    dp = lax.axis_index("dp")
    ex = lax.axis_index("expert")
    x, y = lax.rem(dp, 4), dp // 4
    z, c = ex // 2, lax.rem(ex, 2)
    expert = (z // 4).astype(F32)
    xe, ye = lax.rem((x + 1) // 2, 2), lax.rem((y + 1) // 2, 2)
    bits = (xe, x // 2, ye, y // 2)

    def partner(dims):
        px, py = x, y
        if 0 in dims:
            px = x + 1 - 2 * lax.rem(x, 2)
        if 1 in dims:
            px = 3 - x
        if 2 in dims:
            py = y + 1 - 2 * lax.rem(y, 2)
        if 3 in dims:
            py = 3 - y
        return (py * 4 + px, ex)

    sibling = (dp, z * 2 + 1 - c)
    above = (dp, lax.rem(z + 1, 16) * 2 + c)
    below = (dp, lax.rem(z + 15, 16) * 2 + c)

    def copy(src, dst, send, recv, device):
        return pltpu.make_async_remote_copy(
            src_ref=src, dst_ref=dst, send_sem=send, recv_sem=recv, device_id=device, device_id_type=MESH
        )

    def along_expert(i):
        return (dp, lax.rem(ex + i, 32)), lax.rem(ex + 32 - i, 32)

    def along_dp(i):
        return (lax.rem(dp + i, 16), ex), lax.rem(dp + 16 - i, 16)

    def spread(n, peer, source, table, mine, send, recv):
        def one(i, carry):
            device, _ = peer(i)
            copy(source(i), table.at[mine], send.at[i], recv.at[i], device).start()
            return carry

        lax.fori_loop(1, n, one, 0)

    def gather_wait(n, peer, source, table, send, recv):
        def one(i, carry):
            device, origin = peer(i)
            c = copy(source(i), table.at[origin], send.at[i], recv.at[i], device)
            c.wait_send()
            c.wait_recv()
            return carry

        lax.fori_loop(1, n, one, 0)

    barrier = pltpu.get_barrier_semaphore()

    def greet(i, carry):
        pl.semaphore_signal(barrier, inc=1, device_id=along_expert(i)[0], device_id_type=MESH)
        return carry

    def greet_dp(i, carry):
        pl.semaphore_signal(barrier, inc=1, device_id=along_dp(i)[0], device_id_type=MESH)
        return carry

    lax.fori_loop(1, 32, greet, 0)
    lax.fori_loop(1, 16, greet_dp, 0)

    tb[0, 0, c, 0:64] = x_ref[...]
    tb[0, 0, c, 64:80] = meta_ref[...]
    tb[0, 0, c, 80:144] = d_ref[...]
    a_own = meta_ref[0:8, 0:64].astype(F32)[0:1]
    b_own = meta_ref[8:16, 0:64].astype(F32)[0:1]
    ls[...] = jnp.zeros_like(ls)
    ls[:, 0:64] = dot(rwt_ref[...], x_ref[...], (1, 1))[0:8]
    gp[...] = jnp.zeros_like(gp)
    gap[...] = jnp.zeros_like(gap)
    dd[...] = jnp.zeros_like(dd)

    pl.semaphore_wait(barrier, 46)

    def z_copy(p, u, src, dst):
        low, size = PARTS[p]
        rows = pl.ds(low, size)
        return copy(
            tb.at[u if src is not None else 0, src if src is not None else 0, c, rows],
            tb.at[u, dst, c, rows],
            z_s.at[p, u, dst],
            z_r.at[p, u, dst],
            above if u == 0 else below,
        )

    def b_copy(p, u, j, core):
        low, size = PARTS[p]
        rows = pl.ds(low, size)
        return copy(tb.at[u, j, core, rows], tb.at[u, j, core, rows], b_s.at[p, u, j], b_r.at[p, u, j], sibling)

    for p in (0, 1):
        z_copy(p, 0, None, 1).start()
        z_copy(p, 1, None, 0).start()
        b_copy(p, 0, 0, c).start()
    spread(16, along_dp, lambda i: ls, lr, dp, l_s, l_r)
    lr[dp] = ls[...]
    for e in range(4):
        ph[e * 32 : e * 32 + 32, :] = route(a_own, b_own, float(e)).astype(BF16)

    def z_step(t, p):
        @pl.when(t < STEPS - 1)
        def _():
            z_copy(p, 0, t, t + 1).wait_recv()

            @pl.when(t < STEPS - 2)
            def _():
                z_copy(p, 0, t + 1, t + 2).start()

            b_copy(p, 0, t + 1, c).start()

        @pl.when(t < STEPS)
        def _():
            z_copy(p, 1, t, t).wait_recv()

            @pl.when(t < STEPS - 1)
            def _():
                z_copy(p, 1, t, t + 1).start()

            b_copy(p, 1, t, c).start()

    def z_sent(t, p):
        @pl.when((t > 0) & (t < STEPS))
        def _():
            z_copy(p, 0, t - 1, t).wait_send()

        @pl.when((t > 0) & (t < STEPS + 1))
        def _():
            z_copy(p, 1, t - 1, t - 1).wait_send()

    def info(q):
        order = ORDERS[q]
        return order, tuple(bits[d] for d in order)

    def rs_sem(which, j, q, m):
        return which.at[j, q * 5 + m]

    def rs_copy(j, q, m):
        order, b = info(q)
        if m == 0:
            src, dst = part.at[j, q, pl.ds((1 - b[0]) * 8, 8)], rs0.at[j, q]
            dims = order[:1]
        elif m == 1:
            src, dst = part.at[j, q, pl.ds(b[0] * 8 + (1 - b[1]) * 4, 4)], rs1.at[j, q]
            dims = order[1:2]
        else:
            mask = m - 1
            src = part.at[j, q, pl.ds(b[0] * 8 + b[1] * 4 + local(b, mask), 1)]
            dst = rs2.at[j, q, pl.ds(mask - 1, 1)]
            dims = tuple(d for k, d in enumerate(order[2:]) if mask & (2 >> k))
        return copy(src, dst, rs_sem(rs_s, j, q, m), rs_sem(rs_r, j, q, m), partner(dims))

    def local(b, mask):
        high = 1 - b[2] if mask & 2 else b[2]
        low = 1 - b[3] if mask & 1 else b[3]
        return high * 2 + low

    def ag_copy(j, q, m, arriving=False):
        order, b = info(q)
        if m == 0:
            dims, size = order[:1], 8
            start = ((1 - b[0]) if arriving else b[0]) * 8
        elif m == 1:
            dims, size = order[1:2], 4
            start = b[0] * 8 + ((1 - b[1]) if arriving else b[1]) * 4
        else:
            mask = m - 1
            dims, size = tuple(d for k, d in enumerate(order[2:]) if mask & (2 >> k)), 1
            start = b[0] * 8 + b[1] * 4 + local(b, mask if arriving else 0)
        ref = ag.at[j, q, pl.ds(start, size)]
        return copy(ref, ref, rs_sem(ag_s, j, q, m), rs_sem(ag_r, j, q, m), partner(dims))

    def start_unit(u, j):
        up, down = up_ref[...], down_ref[...]
        xs, ds = [], []
        for core in (0, 1):
            rows = tb.at[u, j, core]
            meta = rows[64:80, 0:64].astype(F32)
            pick = route(meta[0:1], meta[8:9], expert).astype(BF16)
            pb[u, j, core] = pick
            xs.append(dot(pick, rows[0:64], (1, 0)).astype(BF16))
            ds.append(dot(pick, rows[80:144], (1, 0)).astype(BF16))
            ax[j, core * 64 + u * 32 : core * 64 + u * 32 + 32] = xs[core]
            ad[j, core * 64 + u * 32 : core * 64 + u * 32 + 32] = ds[core]
        for a, (rows, weight) in enumerate(((xs, up), (ds, down))):
            q = 2 * u + a
            value = dot(jnp.concatenate(rows, axis=0), weight, (1, 0)).astype(BF16)
            for block in range(16):
                bit = (block >> 3 & 1, block >> 2 & 1, block >> 1 & 1, block & 1)
                spot = sum(bit[d] << (3 - k) for k, d in enumerate(ORDERS[q]))
                half, column = bit[0], bit[1] * 4 + bit[2] * 2 + bit[3]
                part[j, q, spot] = value[half * 32 : half * 32 + 32, column * 128 : column * 128 + 128]
            rs_copy(j, q, 0).start()

    def wait_sibling(u, j):
        for p in (0, 1):
            cp = b_copy(p, u, j, 1 - c)
            cp.wait_send()
            cp.wait_recv()

    def reduce_one(j):
        for q in range(4):
            _, b = info(q)
            rs_copy(j, q, 0).wait_recv()
            near = (1 - b[1]) * 4
            part[j, q, pl.ds(b[0] * 8 + near, 4)] += rs0[j, q, pl.ds(near, 4)]
            rs_copy(j, q, 1).start()
            near = b[1] * 4
            part[j, q, pl.ds(b[0] * 8 + near, 4)] += rs0[j, q, pl.ds(near, 4)]
            rs_copy(j, q, 0).wait_send()

    def reduce_two(j):
        for q in range(4):
            _, b = info(q)
            rs_copy(j, q, 1).wait_recv()
            for mask in (3, 1, 2, 0):
                at = local(b, mask)
                part[j, q, b[0] * 8 + b[1] * 4 + at] += rs1[j, q, at]
                if mask:
                    rs_copy(j, q, mask + 1).start()
            rs_copy(j, q, 1).wait_send()

    def chip_of(u, j):
        return lax.rem(z + 16 - j, 16) if u == 0 else lax.rem(z + j + 1, 16)

    def total(j, q):
        _, b = info(q)
        for mask in (1, 2, 3):
            rs_copy(j, q, mask + 1).wait_recv()
            rs_copy(j, q, mask + 1).wait_send()
        parts = rs2[j, q].astype(F32)
        own = part[j, q, b[0] * 8 + b[1] * 4 + b[2] * 2 + b[3]].astype(F32)
        return own + parts[0] + parts[1] + parts[2]

    def activate(j):
        for u in (0, 1):
            d = chip_of(u, j)
            before = total(j, 2 * u)
            back = total(j, 2 * u + 1)
            meta = tb[u, j, xe, 64:80, 0:64].astype(F32)
            gap_row = gaps[2 * d + xe][:, 0:64]
            gate_row = jnp.where(
                meta[0:1] == expert,
                jax.nn.sigmoid(gap_row),
                jnp.where(meta[8:9] == expert, jax.nn.sigmoid(-gap_row), 0.0),
            )
            gate_row = gate_row.astype(BF16).astype(F32)
            gate = jnp.sum(pb[u, j, xe].astype(F32) * jnp.broadcast_to(gate_row, (32, 64)), axis=1, keepdims=True)
            bell = 0.5 * (1.0 + lax.erf(before * ROOT_HALF))
            active = before * bell
            slope = bell + before * jnp.exp(-0.5 * before * before) * INV_ROOT_TWO_PI
            inner = (gate * back * slope).astype(BF16)
            weighted = (gate * active).astype(BF16)
            product = active.astype(BF16).astype(F32) * back
            for a, tile in ((0, inner), (1, weighted)):
                q = 2 * u + a
                _, b = info(q)
                ag[j, q, b[0] * 8 + b[1] * 4 + b[2] * 2 + b[3]] = tile
                for mask in (3, 1, 2):
                    ag_copy(j, q, mask + 1).start()
            high, low = split(product)
            ones = jnp.ones((16, 128), BF16)
            sums = dot(ones, high, (1, 1)) + dot(ones, low, (1, 1))
            gp[d, :, 0:32] = sums[0:1]

    def gather_one(j):
        for q in range(4):
            for mask in (1, 2, 3):
                ag_copy(j, q, mask + 1, True).wait_recv()
            ag_copy(j, q, 1).start()
            for mask in (1, 2, 3):
                ag_copy(j, q, mask + 1).wait_send()

    def gather_two(j):
        for q in range(4):
            ag_copy(j, q, 1, True).wait_recv()
            ag_copy(j, q, 0).start()
            ag_copy(j, q, 1).wait_send()

    def sx_copy(j):
        return copy(pi.at[j, 1 - c], sx.at[j], sx_s.at[j], sx_r.at[j], sibling)

    def finish_unit(j):
        for q in range(4):
            ag_copy(j, q, 0, True).wait_recv()
            ag_copy(j, q, 0).wait_send()
            u, into = q // 2, (inn, wgt)[q % 2]
            for block in range(16):
                bit = (block >> 3 & 1, block >> 2 & 1, block >> 1 & 1, block & 1)
                spot = sum(bit[d] << (3 - k) for k, d in enumerate(ORDERS[q]))
                row, column = bit[0] * 64 + u * 32, (bit[1] * 4 + bit[2] * 2 + bit[3]) * 128
                into[j, row : row + 32, column : column + 128] = ag[j, q, spot]
        value = dot(inn[j], up_ref[...], (1, 1)).astype(BF16)
        pi[j, 0] = value[0:64]
        pi[j, 1] = value[64:128]
        sx_copy(j).start()

    def ret_copy(u, j):
        device = (dp, chip_of(u, j) * 2 + c)
        return copy(rb.at[j, pl.ds(u * 32, 32)], ret.at[z], ret_s.at[u, j], ret_r.at[u, j], device)

    def return_unit(j):
        sx_copy(j).wait_recv()
        sx_copy(j).wait_send()
        rb[j] = (pi[j, c].astype(F32) + sx[j].astype(F32)).astype(BF16)

        @pl.when(j == 0)
        def _():
            ret[z] = rb[0, 0:32]

        @pl.when(j > 0)
        def _():
            ret_copy(0, j).start()

        ret_copy(1, j).start()

    def tick(t, carry):
        def stage(lag, action):
            @pl.when((t >= lag) & (t < lag + STEPS))
            def _():
                action(t - lag)

        @pl.when(t < STEPS)
        def _():
            wait_sibling(0, t)
            start_unit(0, t)

        z_step(t, 0)
        z_sent(t, 0)

        @pl.when(t == 1)
        def _():
            gather_wait(16, along_dp, lambda i: ls, lr, l_s, l_r)
            logits = jnp.sum(lr[...], axis=0)
            hot = signed_hot(a_own, b_own)[0:8]
            gap[:, 0:64] = jnp.sum(logits[:, 0:64] * hot, axis=0, keepdims=True)
            gaps[ex] = gap[...]
            spread(32, along_expert, lambda i: gap, gaps, ex, gap_s, gap_r)

        @pl.when(t == 3)
        def _():
            gather_wait(32, along_expert, lambda i: gap, gaps, gap_s, gap_r)

        stage(7, return_unit)
        stage(5, gather_two)
        stage(4, gather_one)
        stage(3, activate)

        @pl.when(t == 10)
        def _():
            gpr[dp] = gp[...]
            spread(16, along_dp, lambda i: gp, gpr, dp, gp_s, gp_r)

        stage(2, reduce_two)
        stage(1, reduce_one)
        z_step(t, 1)
        z_sent(t, 1)

        @pl.when(t == 12)
        def _():
            gather_wait(16, along_dp, lambda i: gp, gpr, gp_s, gp_r)
            for half in (0, 1):
                mine = [k for k in range(16) if ((k % 4 + 1) // 2) % 2 == half]
                acc = gpr[mine[0]]
                for k in mine[1:]:
                    acc = acc + gpr[k]
                for k in range(16):
                    gs[2 * k + half] = acc[k].astype(BF16).astype(F32)
            gret[ex] = gs[ex]
            spread(32, along_expert, lambda i: gs.at[along_expert(i)[0][1]], gret, ex, gr_s, gr_r)

        stage(6, finish_unit)

        @pl.when(t < STEPS)
        def _():
            wait_sibling(1, t)
            start_unit(1, t)

        @pl.when(t == 14)
        def _():
            gather_wait(32, along_expert, lambda i: gs.at[along_expert(i)[0][1]], gret, gr_s, gr_r)
            picked = []
            for e in range(4):
                row = gret[8 * e]
                for k in range(1, 8):
                    row = row + gret[8 * e + k]
                row = jnp.broadcast_to(row[:, 0:32], (16, 32))
                picked.append(dot2(row, ph[e * 32 : e * 32 + 32, :], (1, 0))[0:1])
            first = jnp.zeros((1, 64), F32)
            second = jnp.zeros((1, 64), F32)
            for e in range(4):
                first = first + jnp.where(a_own == float(e), picked[e], 0.0)
                second = second + jnp.where(b_own == float(e), picked[e], 0.0)
            row = gap[:, 0:64]
            gate0 = jax.nn.sigmoid(row).astype(BF16).astype(F32)
            gate1 = jax.nn.sigmoid(-row).astype(BF16).astype(F32)
            delta0 = (first * gate0 * (1.0 - gate0)).astype(BF16).astype(F32)
            delta1 = (second * gate1 * (1.0 - gate1)).astype(BF16).astype(F32)
            dd[:, 0:64] = delta0 - delta1
            ddr[ex] = dd[...]
            spread(32, along_expert, lambda i: dd, ddr, ex, dd_s, dd_r)

        return carry

    lax.fori_loop(0, TICKS, tick, 0)

    rows = STEPS * 128
    for source, values, out in ((ax, inn, gu_ref), (ad, wgt, gd_ref)):
        out[...] = dot(source[...].reshape(rows, 384), values[...].reshape(rows, 1024), (0, 0)).astype(BF16)

    gather_wait(32, along_expert, lambda i: dd, ddr, dd_s, dd_r)

    def add_router(k, acc):
        for u in (0, 1):
            d = chip_of(u, k)
            for core in (0, 1):
                meta = tb[u, k, core, 64:80, 0:64].astype(F32)
                grad = signed_hot(meta[0:1], meta[8:9]) * jnp.broadcast_to(ddr[2 * d + core][:, 0:64], (16, 64))
                acc = acc + dot2(grad, tb[u, k, core, 0:64], (1, 0))
        return acc

    gr_ref[...] = lax.fori_loop(0, STEPS, add_router, jnp.zeros((16, 384), F32))

    def returned(j, carry):
        @pl.when(j > 0)
        def _():
            cp = ret_copy(0, j)
            cp.wait_send()
            cp.wait_recv()

        cp = ret_copy(1, j)
        cp.wait_send()
        cp.wait_recv()
        return carry

    lax.fori_loop(0, STEPS, returned, 0)
    sums = []
    for e in range(4):
        acc = ret[4 * e].astype(F32)
        for k in range(1, 4):
            acc = acc + ret[4 * e + k].astype(F32)
        sums.append(acc)
    high, low = split(jnp.concatenate(sums, axis=0))
    pick = ph[...]
    value = d_ref[...].astype(F32) + (dot(pick, high, (0, 0)) + dot(pick, low, (0, 0)))
    high, low = split(signed_hot(a_own, b_own) * jnp.broadcast_to(dd[:, 0:64], (16, 64)))
    weight = rwt_ref[...]
    value = value + (dot(high, weight, (0, 0)) + dot(low, weight, (0, 0)))
    gi_ref[...] = value.astype(BF16)


def local(inputs, grad_out, expert_ids, live_counts, router_weight, up_weight, down_weight):
    live = jnp.arange(64, dtype=jnp.int32)[:, None] < live_counts[0]
    ids = jnp.where(live, expert_ids, -1).astype(BF16).T
    meta = jnp.full((16, 384), -1.0, BF16).at[0, 0:64].set(ids[0]).at[8, 0:64].set(ids[1])
    router = jnp.zeros((16, 384), BF16).at[0:4].set(router_weight.T)
    vmem = pl.BlockSpec(memory_space=pltpu.VMEM)
    dma = pltpu.SemaphoreType.DMA
    grads = jax.ShapeDtypeStruct((384, 1024), BF16)
    grad_inputs, grad_up, grad_down, grad_router = pl.pallas_call(
        kernel,
        out_shape=(jax.ShapeDtypeStruct((64, 384), BF16), grads, grads, jax.ShapeDtypeStruct((16, 384), F32)),
        in_specs=[vmem] * 6,
        out_specs=(vmem,) * 4,
        scratch_shapes=[
            pltpu.VMEM((2, STEPS, 2, ROWS, 384), BF16),
            pltpu.VMEM((2, STEPS, 2, 32, 64), BF16),
            pltpu.VMEM((128, 64), BF16),
            pltpu.VMEM((STEPS, 128, 384), BF16),
            pltpu.VMEM((STEPS, 128, 384), BF16),
            pltpu.VMEM((STEPS, 4, 16, 32, 128), BF16),
            pltpu.VMEM((STEPS, 4, 8, 32, 128), BF16),
            pltpu.VMEM((STEPS, 4, 4, 32, 128), BF16),
            pltpu.VMEM((STEPS, 4, 3, 32, 128), BF16),
            pltpu.VMEM((STEPS, 4, 16, 32, 128), BF16),
            pltpu.VMEM((STEPS, 128, 1024), BF16),
            pltpu.VMEM((STEPS, 128, 1024), BF16),
            pltpu.VMEM((STEPS, 2, 64, 384), BF16),
            pltpu.VMEM((STEPS, 64, 384), BF16),
            pltpu.VMEM((STEPS, 64, 384), BF16),
            pltpu.VMEM((16, 32, 384), BF16),
            pltpu.VMEM((8, 128), F32),
            pltpu.VMEM((16, 8, 128), F32),
            pltpu.VMEM((1, 128), F32),
            pltpu.VMEM((32, 1, 128), F32),
            pltpu.VMEM((16, 1, 128), F32),
            pltpu.VMEM((16, 16, 1, 128), F32),
            pltpu.VMEM((32, 1, 128), F32),
            pltpu.VMEM((32, 1, 128), F32),
            pltpu.VMEM((1, 128), F32),
            pltpu.VMEM((32, 1, 128), F32),
            dma((2, 2, STEPS)), dma((2, 2, STEPS)),
            dma((2, 2, STEPS)), dma((2, 2, STEPS)),
            dma((STEPS, 20)), dma((STEPS, 20)),
            dma((STEPS, 20)), dma((STEPS, 20)),
            dma((STEPS,)), dma((STEPS,)),
            dma((2, STEPS)), dma((2, STEPS)),
            dma((16,)), dma((16,)),
            dma((32,)), dma((32,)),
            dma((16,)), dma((16,)),
            dma((32,)), dma((32,)),
            dma((32,)), dma((32,)),
        ],
        compiler_params=pltpu.CompilerParams(
            collective_id=0, has_side_effects=True, vmem_limit_bytes=56 * 2**20
        ),
        name="moe_backward",
    )(inputs, grad_out, meta, router, up_weight, down_weight)
    return grad_inputs, grad_up, grad_down, grad_router[0:4].T


def solution(mesh):
    placed = (
        P("expert", "dp"),
        P("expert", "dp"),
        P("expert", None),
        P("expert"),
        P("dp", None),
        P("dp", "expert"),
        P("dp", "expert"),
    )
    return jax.shard_map(
        local,
        mesh=mesh,
        in_specs=placed,
        out_specs=(P("expert", "dp"), P("dp", "expert"), P("dp", "expert"), P("dp", None)),
        check_vma=False,
    )
```

time: 426 us -> 129 us (0.30)
  blocking collectives: 188 us -> 0 us
  waiting for transfers between devices: 145 us -> 0 us
  Pallas kernels: 0 us -> 120 us
  starting transfers between devices: 22.4 us -> 0 us
  local copies, waits for them, and re-layouts: 25.7 us -> 7.7 us
  matrix products: 17.8 us -> 0 us
  between operations: 14.9 us -> 1.33 us
  other arithmetic: 12 us -> 0.01 us
    pallas_call x0 -> x1, Pallas kernels: none -> 120 us  [local(): pl.pallas_call(kernel, out_shape=(jax.ShapeDtypeStruct((64, 384), BF16),...]
    psum x2 -> x0, blocking collectives: 111 us -> none  [the longest x1 76.7 us: local(): grad_router = lax.psum(router_term, 'expert')]
    psum x1 -> x0, waiting for transfers between devices: 91.7 us -> none  [local(): lax.psum(back_part.astype(jnp.bfloat16), 'dp').astype(jnp.float32)]
    all_to_all x2 -> x0, blocking collectives: 76.6 us -> none  [the longest x1 61.2 us: local(): lax.all_to_all(send_rows, 'expert', split_axis=0, concat_axis=0, tiled=True)]
    all_to_all x3 -> x0, waiting for transfers between devices: 53.7 us -> none  [the longest x1 42 us: local(): lax.all_to_all(send_grad, 'expert', split_axis=0, concat_axis=0, tiled=True)]
    gather x8 -> x0, local copies, waits for them, and re-layouts: 23 us -> none  [the longest x2 6.64 us: local(): send_pick = jnp.take(slot_pick, expert_slot, axis=0)]
    all_to_all x3 -> x0, starting transfers between devices: 22.3 us -> none  [the longest x1 13.2 us: local(): lax.all_to_all(gate_part.astype(jnp.bfloat16), 'expert', split_axis=0, co...]
    dot_general x8 -> x0, matrix products: 17.8 us -> none  [the longest x1 4.18 us: local(): lax.dot_general(rows_grad, weighted, contract_rows, preferred_element_typ...]
  transfers between devices with their start and end apart: 4 -> 0, of which waited for: 3 -> 0; matrix products, arithmetic and copies ran while one was open for 3% -> 0% of each run, Pallas kernels for 0% -> 0%
where the time goes in v1:
time: 129 us
  Pallas kernels  120 us (93%)
  local copies, waits for them, and re-layouts  7.7 us (6%)
  between operations  1.33 us (1%)
    pallas_call x1, Pallas kernels, local(): pl.pallas_call(kernel, out_shape=(jax.ShapeDtypeStruct((64, 384), BF16),...  120 us
    unnamed x11, local copies, waits for them, and re-layouts  5.6 us

profile of v1, /device:TPU:1, one launch (start us, length us, event | category | flops | bytes accessed | tf_op | source)
XLA Modules:
  0.0 129.0 jit_solution(11283995625409820751)
XLA Ops:
  1.3 0.0 copy-start.3
  1.3 0.7 copy-done.3
  2.0 0.0 copy-start.2
  2.0 0.2 scatter.11.meta_ref
  2.2 0.5 copy-done.2
  2.7 0.0 copy-start.1
  2.7 0.6 scatter.14.rwt_ref
  3.3 0.0 copy-done.1
  3.3 120.0 %moe_backward.1 = (bf16[64,384]{1,0:T(8,128)(2,1)}, bf16[384,1024]{1,0:T(8,128)(2,1)}, bf16[384,1024]{1,0:T(8,128)(2,1)}, f32[16,384]{1,0:T(8,128)}) custom-call(bf16[64,384]{1,0:T(8,128)(2,1)} %x_ref.1, bf16[64,384]{1,0:T(8,128)(2,1)} %d_ref.1, bf16[16,384]{1,0:T(8,128)(2,1)} %copy-done.1, bf16[16,384]{1,0:T(8,128)(2,1)} %scatter.14.rwt_ref, ...), custom_call_target="tpu_custom_call" | custom-call | tf_op jit(solution)/shard_map/moe_backward/pallas_call | solution.py:523
  123.3 1.3 %slice_bitcast_fusion = f32[384,4]{0,1:T(4,128)} fusion(f32[16,384]{1,0:T(8,128)} %get-tuple-element.47), kind=kLoop, calls=%fused_computation | loop fusion | bytes 12288 | tf_op jit(solution)/shard_map/transpose | solution.py:572
  124.6 1.4 %copy.16 = bf16[64,384]{1,0:T(8,128)(2,1)} copy(bf16[64,384]{1,0:T(8,128)(2,1)} %get-tuple-element.54) | data formatting | bytes 98304
  126.0 0.0 copy-start
  126.0 2.1 %copy.17 = bf16[384,1024]{1,0:T(8,128)(2,1)} copy(bf16[384,1024]{1,0:T(8,128)(2,1)} %get-tuple-element.55) | data formatting | bytes 1572864
  128.1 0.0 copy-done
  128.1 0.9 copy.18
  (4 shorter events, 0.0 us)
Async XLA Ops:
  1.3 0.7 copy-start.3
  2.0 0.7 copy-start.2
  2.7 0.6 copy-start.1
  126.0 2.1 %copy-start = (bf16[384,1024]{1,0:T(8,128)(2,1)S(1)}, bf16[384,1024]{1,0:T(8,128)(2,1)}, u32[]{:S(2)}) copy-start(bf16[384,1024]{1,0:T(8,128)(2,1)} %get-tuple-element.56) | copy-start | bytes 2359300

commit v2 on v1

--- a/solution.py
+++ b/solution.py
@@ -32,14 +32,20 @@
     return dot(high, b, contract) + dot(low, b, contract)
 
 
-def route(a_row, b_row, expert):
-    hit = jnp.where((a_row == expert) | (b_row == expert), 1.0, 0.0)
+def route(pairs):
+    row = lax.broadcasted_iota(jnp.int32, (16, 64), 0)
+    hits = [jnp.where((a == e) | (b == e), 1.0, 0.0) for a, b, e in pairs]
+    table = jnp.zeros((16, 64), F32)
+    for k, hit in enumerate(hits):
+        table = jnp.where(row == k, jnp.broadcast_to(hit, (16, 64)), table)
     upper = lax.broadcasted_iota(jnp.int32, (64, 64), 0) < lax.broadcasted_iota(jnp.int32, (64, 64), 1)
-    rank = dot(
-        jnp.broadcast_to(hit, (16, 64)).astype(BF16), jnp.where(upper, 1.0, 0.0).astype(BF16), (1, 0)
-    )[0:1]
+    rank = dot(table.astype(BF16), jnp.where(upper, 1.0, 0.0).astype(BF16), (1, 0))
     slot = lax.broadcasted_iota(jnp.int32, (32, 64), 0).astype(F32)
-    return jnp.where(slot == jnp.broadcast_to(rank, (32, 64)), jnp.broadcast_to(hit, (32, 64)), 0.0)
+    picks = []
+    for k, hit in enumerate(hits):
+        at = jnp.broadcast_to(rank[k : k + 1], (32, 64))
+        picks.append(jnp.where(slot == at, jnp.broadcast_to(hit, (32, 64)), 0.0).astype(BF16))
+    return picks
 
 
 def signed_hot(a_row, b_row):
@@ -50,12 +56,12 @@
 
 
 def kernel(
-    x_ref, d_ref, meta_ref, rwt_ref, up_ref, down_ref,
-    gi_ref, gu_ref, gd_ref, gr_ref,
-    tb, pb, ph, ax, ad, part, rs0, rs1, rs2, ag, inn, wgt, pi, sx, rb, ret,
+    x_hbm, d_hbm, ids_ref, live_ref, rwt_ref, up_hbm, down_hbm,
+    gi_hbm, gu_hbm, gd_hbm, gr_hbm,
+    up_ref, down_ref, rw, gi, gu, gd, gr, tb, pb, ph, ax, ad, part, rs0, rs1, rs2, ag, inn, wgt, pi, sx, rb, ret,
     ls, lr, gap, gaps, gp, gpr, gs, gret, dd, ddr,
     z_s, z_r, b_s, b_r, rs_s, rs_r, ag_s, ag_r, sx_s, sx_r, ret_s, ret_r,
-    l_s, l_r, gap_s, gap_r, gp_s, gp_r, gr_s, gr_r, dd_s, dd_r,
+    l_s, l_r, gap_s, gap_r, gp_s, gp_r, gr_s, gr_r, dd_s, dd_r, in_s, out_s,
 ):
     dp = lax.axis_index("dp")
     ex = lax.axis_index("expert")
@@ -110,6 +116,19 @@
 
         lax.fori_loop(1, n, one, 0)
 
+    loads = [
+        pltpu.make_async_copy(src, dst, in_s.at[k])
+        for k, (src, dst) in enumerate(
+            (
+                (x_hbm, tb.at[0, 0, c, pl.ds(0, 64)]),
+                (d_hbm, tb.at[0, 0, c, pl.ds(80, 64)]),
+                (up_hbm, up_ref),
+                (down_hbm, down_ref),
+            )
+        )
+    ]
+    for load in loads:
+        load.start()
     barrier = pltpu.get_barrier_semaphore()
 
     def greet(i, carry):
@@ -123,13 +142,20 @@
     lax.fori_loop(1, 32, greet, 0)
     lax.fori_loop(1, 16, greet_dp, 0)
 
-    tb[0, 0, c, 0:64] = x_ref[...]
-    tb[0, 0, c, 64:80] = meta_ref[...]
-    tb[0, 0, c, 80:144] = d_ref[...]
-    a_own = meta_ref[0:8, 0:64].astype(F32)[0:1]
-    b_own = meta_ref[8:16, 0:64].astype(F32)[0:1]
+    ids = ids_ref[...].astype(F32)
+    alive = lax.broadcasted_iota(jnp.int32, (1, 64), 1) < live_ref[0]
+    a_own = jnp.where(alive, ids[0:1], -1.0)
+    b_own = jnp.where(alive, ids[1:2], -1.0)
+    tb[0, 0, c, 64:80] = jnp.zeros((16, 384), BF16)
+    low_half = lax.broadcasted_iota(jnp.int32, (16, 64), 0) < 8
+    both = jnp.where(low_half, jnp.broadcast_to(a_own, (16, 64)), jnp.broadcast_to(b_own, (16, 64)))
+    tb[0, 0, c, 64:80, 0:64] = both.astype(BF16)
+    rw[...] = jnp.zeros_like(rw)
+    rw[0:4] = rwt_ref[...]
     ls[...] = jnp.zeros_like(ls)
-    ls[:, 0:64] = dot(rwt_ref[...], x_ref[...], (1, 1))[0:8]
+    for load in loads[0:2]:
+        load.wait()
+    ls[:, 0:64] = dot(rw[...], tb[0, 0, c, 0:64], (1, 1))[0:8]
     gp[...] = jnp.zeros_like(gp)
     gap[...] = jnp.zeros_like(gap)
     dd[...] = jnp.zeros_like(dd)
@@ -158,8 +184,8 @@
         b_copy(p, 0, 0, c).start()
     spread(16, along_dp, lambda i: ls, lr, dp, l_s, l_r)
     lr[dp] = ls[...]
-    for e in range(4):
-        ph[e * 32 : e * 32 + 32, :] = route(a_own, b_own, float(e)).astype(BF16)
+    for e, pick in enumerate(route([(a_own, b_own, float(e)) for e in range(4)])):
+        ph[e * 32 : e * 32 + 32, :] = pick
 
     def z_step(t, p):
         @pl.when(t < STEPS - 1)
@@ -233,27 +259,33 @@
         ref = ag.at[j, q, pl.ds(start, size)]
         return copy(ref, ref, rs_sem(ag_s, j, q, m), rs_sem(ag_r, j, q, m), partner(dims))
 
-    def start_unit(u, j):
-        up, down = up_ref[...], down_ref[...]
-        xs, ds = [], []
-        for core in (0, 1):
-            rows = tb.at[u, j, core]
-            meta = rows[64:80, 0:64].astype(F32)
-            pick = route(meta[0:1], meta[8:9], expert).astype(BF16)
+    def start_units(j):
+        keys = [(u, core) for core in (0, 1) for u in (0, 1)]
+        for u in (0, 1):
+            wait_sibling(u, j)
+        pairs = []
+        for u, core in keys:
+            meta = tb[u, j, core, 64:80, 0:64].astype(F32)
+            pairs.append((meta[0:1], meta[8:9], expert))
+        picks = route(pairs)
+        for (u, core), pick in zip(keys, picks):
             pb[u, j, core] = pick
-            xs.append(dot(pick, rows[0:64], (1, 0)).astype(BF16))
-            ds.append(dot(pick, rows[80:144], (1, 0)).astype(BF16))
-            ax[j, core * 64 + u * 32 : core * 64 + u * 32 + 32] = xs[core]
-            ad[j, core * 64 + u * 32 : core * 64 + u * 32 + 32] = ds[core]
-        for a, (rows, weight) in enumerate(((xs, up), (ds, down))):
-            q = 2 * u + a
-            value = dot(jnp.concatenate(rows, axis=0), weight, (1, 0)).astype(BF16)
-            for block in range(16):
-                bit = (block >> 3 & 1, block >> 2 & 1, block >> 1 & 1, block & 1)
-                spot = sum(bit[d] << (3 - k) for k, d in enumerate(ORDERS[q]))
-                half, column = bit[0], bit[1] * 4 + bit[2] * 2 + bit[3]
-                part[j, q, spot] = value[half * 32 : half * 32 + 32, column * 128 : column * 128 + 128]
-            rs_copy(j, q, 0).start()
+        for a, (low, weight, keep) in enumerate(((0, up_ref, ax), (80, down_ref, ad))):
+            rows = [
+                dot(pick, tb[u, j, core, low : low + 64], (1, 0)).astype(BF16)
+                for (u, core), pick in zip(keys, picks)
+            ]
+            rows = jnp.concatenate(rows, axis=0)
+            keep[j] = rows
+            value = dot(rows, weight[...], (1, 0)).astype(BF16)
+            for u in (0, 1):
+                q = 2 * u + a
+                for block in range(16):
+                    bit = (block >> 3 & 1, block >> 2 & 1, block >> 1 & 1, block & 1)
+                    spot = sum(bit[d] << (3 - k) for k, d in enumerate(ORDERS[q]))
+                    row, column = bit[0] * 64 + u * 32, (bit[1] * 4 + bit[2] * 2 + bit[3]) * 128
+                    part[j, q, spot] = value[row : row + 32, column : column + 128]
+                rs_copy(j, q, 0).start()
 
     def wait_sibling(u, j):
         for p in (0, 1):
@@ -288,43 +320,51 @@
 
     def total(j, q):
         _, b = info(q)
-        for mask in (1, 2, 3):
-            rs_copy(j, q, mask + 1).wait_recv()
-            rs_copy(j, q, mask + 1).wait_send()
         parts = rs2[j, q].astype(F32)
         own = part[j, q, b[0] * 8 + b[1] * 4 + b[2] * 2 + b[3]].astype(F32)
         return own + parts[0] + parts[1] + parts[2]
 
     def activate(j):
+        for q in range(4):
+            for mask in (1, 2, 3):
+                rs_copy(j, q, mask + 1).wait_recv()
+        before = jnp.concatenate([total(j, 0), total(j, 2)], axis=0)
+        back = jnp.concatenate([total(j, 1), total(j, 3)], axis=0)
+        gates = []
         for u in (0, 1):
-            d = chip_of(u, j)
-            before = total(j, 2 * u)
-            back = total(j, 2 * u + 1)
             meta = tb[u, j, xe, 64:80, 0:64].astype(F32)
-            gap_row = gaps[2 * d + xe][:, 0:64]
+            gap_row = gaps[2 * chip_of(u, j) + xe][:, 0:64]
             gate_row = jnp.where(
                 meta[0:1] == expert,
                 jax.nn.sigmoid(gap_row),
                 jnp.where(meta[8:9] == expert, jax.nn.sigmoid(-gap_row), 0.0),
             )
             gate_row = gate_row.astype(BF16).astype(F32)
-            gate = jnp.sum(pb[u, j, xe].astype(F32) * jnp.broadcast_to(gate_row, (32, 64)), axis=1, keepdims=True)
-            bell = 0.5 * (1.0 + lax.erf(before * ROOT_HALF))
-            active = before * bell
-            slope = bell + before * jnp.exp(-0.5 * before * before) * INV_ROOT_TWO_PI
-            inner = (gate * back * slope).astype(BF16)
-            weighted = (gate * active).astype(BF16)
-            product = active.astype(BF16).astype(F32) * back
-            for a, tile in ((0, inner), (1, weighted)):
-                q = 2 * u + a
-                _, b = info(q)
-                ag[j, q, b[0] * 8 + b[1] * 4 + b[2] * 2 + b[3]] = tile
-                for mask in (3, 1, 2):
-                    ag_copy(j, q, mask + 1).start()
-            high, low = split(product)
-            ones = jnp.ones((16, 128), BF16)
-            sums = dot(ones, high, (1, 1)) + dot(ones, low, (1, 1))
-            gp[d, :, 0:32] = sums[0:1]
+            gates.append(
+                jnp.sum(pb[u, j, xe].astype(F32) * jnp.broadcast_to(gate_row, (32, 64)), axis=1, keepdims=True)
+            )
+        gate = jnp.concatenate(gates, axis=0)
+        bell = 0.5 * (1.0 + lax.erf(before * ROOT_HALF))
+        active = before * bell
+        slope = bell + before * jnp.exp(-0.5 * before * before) * INV_ROOT_TWO_PI
+        inner = (gate * back * slope).astype(BF16)
+        weighted = (gate * active).astype(BF16)
+        product = active.astype(BF16).astype(F32) * back
+        high, low = split(product)
+        ones = jnp.ones((16, 128), BF16)
+        sums = dot(ones, high, (1, 1)) + dot(ones, low, (1, 1))
+        for q in range(4):
+            _, b = info(q)
+            u, tile = q // 2, (inner, weighted)[q % 2]
+            ag[j, q, b[0] * 8 + b[1] * 4 + b[2] * 2 + b[3]] = tile[u * 32 : u * 32 + 32]
+        for q in range(4):
+            for mask in (3, 1, 2):
+                ag_copy(j, q, mask + 1).start()
+        for u in (0, 1):
+            gp[chip_of(u, j), :, 0:32] = sums[0:1, u * 32 : u * 32 + 32]
+        for q in range(4):
+            for mask in (1, 2, 3):
+                rs_copy(j, q, mask + 1).wait_send()
 
     def gather_one(j):
         for q in range(4):
@@ -383,15 +423,13 @@
             def _():
                 action(t - lag)
 
-        @pl.when(t < STEPS)
-        def _():
-            wait_sibling(0, t)
-            start_unit(0, t)
-
-        z_step(t, 0)
-        z_sent(t, 0)
-
-        @pl.when(t == 1)
+        stage(0, start_units)
+        z_step(t + 1, 0)
+        z_sent(t + 1, 0)
+        stage(1, reduce_one)
+        stage(2, reduce_two)
+
+        @pl.when(t == 0)
         def _():
             gather_wait(16, along_dp, lambda i: ls, lr, l_s, l_r)
             logits = jnp.sum(lr[...], axis=0)
@@ -404,22 +442,21 @@
         def _():
             gather_wait(32, along_expert, lambda i: gap, gaps, gap_s, gap_r)
 
-        stage(7, return_unit)
-        stage(5, gather_two)
-        stage(4, gather_one)
         stage(3, activate)
+        z_step(t + 1, 1)
+        z_sent(t + 1, 1)
 
         @pl.when(t == 10)
         def _():
             gpr[dp] = gp[...]
             spread(16, along_dp, lambda i: gp, gpr, dp, gp_s, gp_r)
 
-        stage(2, reduce_two)
-        stage(1, reduce_one)
-        z_step(t, 1)
-        z_sent(t, 1)
-
-        @pl.when(t == 12)
+        stage(4, gather_one)
+        stage(5, gather_two)
+        stage(6, finish_unit)
+        stage(7, return_unit)
+
+        @pl.when(t == 11)
         def _():
             gather_wait(16, along_dp, lambda i: gp, gpr, gp_s, gp_r)
             for half in (0, 1):
@@ -432,14 +469,7 @@
             gret[ex] = gs[ex]
             spread(32, along_expert, lambda i: gs.at[along_expert(i)[0][1]], gret, ex, gr_s, gr_r)
 
-        stage(6, finish_unit)
-
-        @pl.when(t < STEPS)
-        def _():
-            wait_sibling(1, t)
-            start_unit(1, t)
-
-        @pl.when(t == 14)
+        @pl.when(t == 13)
         def _():
             gather_wait(32, along_expert, lambda i: gs.at[along_expert(i)[0][1]], gret, gr_s, gr_r)
             picked = []
@@ -465,11 +495,20 @@
 
         return carry
 
+    for load in loads[2:]:
+        load.wait()
+    for p in (0, 1):
+        z_step(0, p)
     lax.fori_loop(0, TICKS, tick, 0)
 
     rows = STEPS * 128
-    for source, values, out in ((ax, inn, gu_ref), (ad, wgt, gd_ref)):
+    stores = [
+        pltpu.make_async_copy(src, dst, out_s.at[k])
+        for k, (src, dst) in enumerate(((gu, gu_hbm), (gd, gd_hbm), (gr, gr_hbm), (gi, gi_hbm)))
+    ]
+    for k, (source, values, out) in enumerate(((ax, inn, gu), (ad, wgt, gd))):
         out[...] = dot(source[...].reshape(rows, 384), values[...].reshape(rows, 1024), (0, 0)).astype(BF16)
+        stores[k].start()
 
     gather_wait(32, along_expert, lambda i: dd, ddr, dd_s, dd_r)
 
@@ -482,7 +521,8 @@
                 acc = acc + dot2(grad, tb[u, k, core, 0:64], (1, 0))
         return acc
 
-    gr_ref[...] = lax.fori_loop(0, STEPS, add_router, jnp.zeros((16, 384), F32))
+    gr[...] = lax.fori_loop(0, STEPS, add_router, jnp.zeros((16, 384), F32))[0:4]
+    stores[2].start()
 
     def returned(j, carry):
         @pl.when(j > 0)
@@ -505,27 +545,52 @@
         sums.append(acc)
     high, low = split(jnp.concatenate(sums, axis=0))
     pick = ph[...]
-    value = d_ref[...].astype(F32) + (dot(pick, high, (0, 0)) + dot(pick, low, (0, 0)))
+    value = tb[0, 0, c, 80:144].astype(F32) + (dot(pick, high, (0, 0)) + dot(pick, low, (0, 0)))
     high, low = split(signed_hot(a_own, b_own) * jnp.broadcast_to(dd[:, 0:64], (16, 64)))
-    weight = rwt_ref[...]
+    weight = rw[...]
     value = value + (dot(high, weight, (0, 0)) + dot(low, weight, (0, 0)))
-    gi_ref[...] = value.astype(BF16)
+    gi[...] = value.astype(BF16)
+    stores[3].start()
+    for store in stores:
+        store.wait()
+
+
+def place(*refs):
+    sources, outs, held, (arrive, leave) = refs[:4], refs[4:8], refs[8:12], refs[12:]
+    pieces = [(1, 0, 192), (1, 192, 192), (2, 0, 192), (2, 192, 192), (0, 0, 64), (3, 0, 4)]
+    loads, stores = [], []
+    for n, (k, low, size) in enumerate(pieces):
+        rows = pl.ds(low, size)
+        loads.append(pltpu.make_async_copy(sources[k].at[rows], held[k].at[rows], arrive.at[n]))
+        stores.append(pltpu.make_async_copy(held[k].at[rows], outs[k].at[rows], leave.at[n]))
+    for load in loads:
+        load.start()
+    for load, store in zip(loads, stores):
+        load.wait()
+        store.start()
+    for store in stores:
+        store.wait()
 
 
 def local(inputs, grad_out, expert_ids, live_counts, router_weight, up_weight, down_weight):
-    live = jnp.arange(64, dtype=jnp.int32)[:, None] < live_counts[0]
-    ids = jnp.where(live, expert_ids, -1).astype(BF16).T
-    meta = jnp.full((16, 384), -1.0, BF16).at[0, 0:64].set(ids[0]).at[8, 0:64].set(ids[1])
-    router = jnp.zeros((16, 384), BF16).at[0:4].set(router_weight.T)
     vmem = pl.BlockSpec(memory_space=pltpu.VMEM)
     dma = pltpu.SemaphoreType.DMA
+    anywhere = pl.BlockSpec(memory_space=pl.ANY)
     grads = jax.ShapeDtypeStruct((384, 1024), BF16)
-    grad_inputs, grad_up, grad_down, grad_router = pl.pallas_call(
+    shapes = (jax.ShapeDtypeStruct((64, 384), BF16), grads, grads, jax.ShapeDtypeStruct((4, 384), F32))
+    results = pl.pallas_call(
         kernel,
-        out_shape=(jax.ShapeDtypeStruct((64, 384), BF16), grads, grads, jax.ShapeDtypeStruct((16, 384), F32)),
-        in_specs=[vmem] * 6,
-        out_specs=(vmem,) * 4,
+        out_shape=shapes,
+        in_specs=[anywhere, anywhere, vmem, pl.BlockSpec(memory_space=pltpu.SMEM), vmem, anywhere, anywhere],
+        out_specs=(anywhere,) * 4,
         scratch_shapes=[
+            pltpu.VMEM((384, 1024), BF16),
+            pltpu.VMEM((384, 1024), BF16),
+            pltpu.VMEM((16, 384), BF16),
+            pltpu.VMEM((64, 384), BF16),
+            pltpu.VMEM((384, 1024), BF16),
+            pltpu.VMEM((384, 1024), BF16),
+            pltpu.VMEM((4, 384), F32),
             pltpu.VMEM((2, STEPS, 2, ROWS, 384), BF16),
             pltpu.VMEM((2, STEPS, 2, 32, 64), BF16),
             pltpu.VMEM((128, 64), BF16),
@@ -563,13 +628,22 @@
             dma((16,)), dma((16,)),
             dma((32,)), dma((32,)),
             dma((32,)), dma((32,)),
+            dma((4,)), dma((4,)),
         ],
         compiler_params=pltpu.CompilerParams(
             collective_id=0, has_side_effects=True, vmem_limit_bytes=56 * 2**20
         ),
         name="moe_backward",
-    )(inputs, grad_out, meta, router, up_weight, down_weight)
-    return grad_inputs, grad_up, grad_down, grad_router[0:4].T
+    )(inputs, grad_out, expert_ids.T, live_counts, router_weight.T, up_weight, down_weight)
+    grad_inputs, grad_up, grad_down, grad_router = pl.pallas_call(
+        place,
+        out_shape=shapes,
+        in_specs=[anywhere] * 4,
+        out_specs=(anywhere,) * 4,
+        scratch_shapes=[pltpu.VMEM(shape.shape, shape.dtype) for shape in shapes] + [dma((6,)), dma((6,))],
+        name="place",
+    )(*results)
+    return grad_inputs, grad_up, grad_down, grad_router.T
 
 
 def solution(mesh):

time: 129 us -> 112 us (0.87)
  Pallas kernels: 120 us -> 111 us
  local copies, waits for them, and re-layouts: 7.7 us -> 0 us
    pallas_call x1 -> x2, Pallas kernels: 120 us -> 111 us  [the longest x1 108 us: local(): pl.pallas_call(kernel, out_shape=shapes, in_specs=[anywhere, anywhere, vm...]
    unnamed x11 -> x0, local copies, waits for them, and re-layouts: 5.6 us -> none
    transpose x1 -> x0, local copies, waits for them, and re-layouts: 1.3 us -> none  [local(): return (grad_inputs, grad_up, grad_down, grad_router[0:4].T)]
where the time goes in v2:
time: 112 us
  Pallas kernels  111 us (99%)
  between operations  1.29 us (1%)
    pallas_call x1, Pallas kernels, local(): pl.pallas_call(kernel, out_shape=shapes, in_specs=[anywhere, anywhere, vm...  108 us
    pallas_call x1, Pallas kernels, local(): pl.pallas_call(place, out_shape=shapes, in_specs=[anywhere] * 4, out_spec...  2.24 us

profile of v2, /device:TPU:1, one launch (start us, length us, event | category | flops | bytes accessed | tf_op | source)
XLA Modules:
  0.0 111.8 jit_solution(646948382374687481)
XLA Ops:
  1.3 108.3 %moe_backward.1 = (bf16[64,384]{1,0:T(8,128)(2,1)}, bf16[384,1024]{1,0:T(8,128)(2,1)}, bf16[384,1024]{1,0:T(8,128)(2,1)}, f32[4,384]{1,0:T(4,128)}) custom-call(bf16[64,384]{1,0:T(8,128)(2,1)} %x_hbm.1, bf16[64,384]{1,0:T(8,128)(2,1)} %d_hbm.1, s32[2,64]{1,0:T(2,128)} %bitcast.4, s32[1]{0:T(128)S(6)} %copy.11.live_ref, bf16[4,384]{1,0:T(4,128)(2,1)} %bitcast.3, ...), custom_call_target="tpu_custom_call" | custom-call | tf_op jit(solution)/shard_map/moe_backward/pallas_call | solution.py:581
  109.6 2.2 %place.1 = (bf16[64,384]{1,0:T(8,128)(2,1)}, bf16[384,1024]{1,0:T(8,128)(2,1)}, bf16[384,1024]{1,0:T(8,128)(2,1)}, f32[4,384]{1,0:T(4,128)}) custom-call(bf16[64,384]{1,0:T(8,128)(2,1)} %get-tuple-element.12.refs_0_, bf16[384,1024]{1,0:T(8,128)(2,1)} %get-tuple-element.13.refs_1_, bf16[384,1024]{1,0:T(8,128)(2,1)} %get-tuple-element.14.refs_2_, ...), custom_call_target="tpu_custom_call" | custom-call | tf_op jit(solution)/shard_map/place/pallas_call | solution.py:638

commit v3 on v2

--- a/solution.py
+++ b/solution.py
@@ -131,15 +131,12 @@
         load.start()
     barrier = pltpu.get_barrier_semaphore()
 
-    def greet(i, carry):
-        pl.semaphore_signal(barrier, inc=1, device_id=along_expert(i)[0], device_id_type=MESH)
-        return carry
-
     def greet_dp(i, carry):
         pl.semaphore_signal(barrier, inc=1, device_id=along_dp(i)[0], device_id_type=MESH)
         return carry
 
-    lax.fori_loop(1, 32, greet, 0)
+    for device in (above, below, sibling):
+        pl.semaphore_signal(barrier, inc=1, device_id=device, device_id_type=MESH)
     lax.fori_loop(1, 16, greet_dp, 0)
 
     ids = ids_ref[...].astype(F32)
@@ -160,7 +157,7 @@
     gap[...] = jnp.zeros_like(gap)
     dd[...] = jnp.zeros_like(dd)
 
-    pl.semaphore_wait(barrier, 46)
+    pl.semaphore_wait(barrier, 18)
 
     def z_copy(p, u, src, dst):
         low, size = PARTS[p]
@@ -324,7 +321,20 @@
         own = part[j, q, b[0] * 8 + b[1] * 4 + b[2] * 2 + b[3]].astype(F32)
         return own + parts[0] + parts[1] + parts[2]
 
+    def gap_copy(u, j, core):
+        target = lax.rem(z + j, 16) if u == 0 else lax.rem(z + 15 - j, 16)
+        return copy(gap, gaps.at[ex], gap_s.at[u, j, core], gap_r.at[u, j], (dp, target * 2 + core))
+
+    def gap_wait(u, j):
+        origin = chip_of(u, j) * 2 + xe
+        copy(gap, gaps.at[origin], gap_s.at[u, j, 0], gap_r.at[u, j], sibling).wait_recv()
+
     def activate(j):
+        @pl.when((j > 0) | (c != xe))
+        def _():
+            gap_wait(0, j)
+
+        gap_wait(1, j)
         for q in range(4):
             for mask in (1, 2, 3):
                 rs_copy(j, q, mask + 1).wait_recv()
@@ -436,11 +446,18 @@
             hot = signed_hot(a_own, b_own)[0:8]
             gap[:, 0:64] = jnp.sum(logits[:, 0:64] * hot, axis=0, keepdims=True)
             gaps[ex] = gap[...]
-            spread(32, along_expert, lambda i: gap, gaps, ex, gap_s, gap_r)
-
-        @pl.when(t == 3)
-        def _():
-            gather_wait(32, along_expert, lambda i: gap, gaps, gap_s, gap_r)
+
+        @pl.when((c == xe) & (t < STEPS))
+        def _():
+            for core in (0, 1):
+                @pl.when((t > 0) | (core != c))
+                def _():
+                    gap_copy(0, t, core).start()
+
+        @pl.when((c == xe) & (t > 0) & (t < STEPS + 1))
+        def _():
+            for core in (0, 1):
+                gap_copy(1, t - 1, core).start()
 
         stage(3, activate)
         z_step(t + 1, 1)
@@ -500,6 +517,19 @@
     for p in (0, 1):
         z_step(0, p)
     lax.fori_loop(0, TICKS, tick, 0)
+
+    @pl.when(c == xe)
+    def _():
+        def sent(j, carry):
+            for core in (0, 1):
+                @pl.when((j > 0) | (core != c))
+                def _():
+                    gap_copy(0, j, core).wait_send()
+
+                gap_copy(1, j, core).wait_send()
+            return carry
+
+        lax.fori_loop(0, STEPS, sent, 0)
 
     rows = STEPS * 128
     stores = [
@@ -624,7 +654,7 @@
             dma((STEPS,)), dma((STEPS,)),
             dma((2, STEPS)), dma((2, STEPS)),
             dma((16,)), dma((16,)),
-            dma((32,)), dma((32,)),
+            dma((2, STEPS, 2)), dma((2, STEPS)),
             dma((16,)), dma((16,)),
             dma((32,)), dma((32,)),
             dma((32,)), dma((32,)),

time: 112 us -> 108 us (0.964)
  Pallas kernels: 111 us -> 106 us
    pallas_call x1, Pallas kernels: 108 us -> 104 us  [local(): pl.pallas_call(kernel, out_shape=shapes, in_specs=[anywhere, anywhere, vm...]
where the time goes in v3:
time: 108 us
  Pallas kernels  106 us (98%)
  between operations  1.29 us (1%)
    pallas_call x1, Pallas kernels, local(): pl.pallas_call(kernel, out_shape=shapes, in_specs=[anywhere, anywhere, vm...  104 us
    pallas_call x1, Pallas kernels, local(): pl.pallas_call(place, out_shape=shapes, in_specs=[anywhere] * 4, out_spec...  2.24 us

profile of v3, /device:TPU:1, one launch (start us, length us, event | category | flops | bytes accessed | tf_op | source)
XLA Modules:
  0.0 107.6 jit_solution(15667456898195316161)
XLA Ops:
  1.3 104.1 %moe_backward.1 = (bf16[64,384]{1,0:T(8,128)(2,1)}, bf16[384,1024]{1,0:T(8,128)(2,1)}, bf16[384,1024]{1,0:T(8,128)(2,1)}, f32[4,384]{1,0:T(4,128)}) custom-call(bf16[64,384]{1,0:T(8,128)(2,1)} %x_hbm.1, bf16[64,384]{1,0:T(8,128)(2,1)} %d_hbm.1, s32[2,64]{1,0:T(2,128)} %bitcast.4, s32[1]{0:T(128)S(6)} %copy.11.live_ref, bf16[4,384]{1,0:T(4,128)(2,1)} %bitcast.3, ...), custom_call_target="tpu_custom_call" | custom-call | tf_op jit(solution)/shard_map/moe_backward/pallas_call | solution.py:611
  105.4 2.2 %place.1 = (bf16[64,384]{1,0:T(8,128)(2,1)}, bf16[384,1024]{1,0:T(8,128)(2,1)}, bf16[384,1024]{1,0:T(8,128)(2,1)}, f32[4,384]{1,0:T(4,128)}) custom-call(bf16[64,384]{1,0:T(8,128)(2,1)} %get-tuple-element.12.refs_0_, bf16[384,1024]{1,0:T(8,128)(2,1)} %get-tuple-element.13.refs_1_, bf16[384,1024]{1,0:T(8,128)(2,1)} %get-tuple-element.14.refs_2_, ...), custom_call_target="tpu_custom_call" | custom-call | tf_op jit(solution)/shard_map/place/pallas_call | solution.py:668

commit v4 on v3

--- a/solution.py
+++ b/solution.py
@@ -436,6 +436,8 @@
         stage(0, start_units)
         z_step(t + 1, 0)
         z_sent(t + 1, 0)
+        z_step(t + 1, 1)
+        z_sent(t + 1, 1)
         stage(1, reduce_one)
         stage(2, reduce_two)
 
@@ -460,8 +462,6 @@
                 gap_copy(1, t - 1, core).start()
 
         stage(3, activate)
-        z_step(t + 1, 1)
-        z_sent(t + 1, 1)
 
         @pl.when(t == 10)
         def _():

time: 108 us -> 107 us (level)
  Pallas kernels: 106 us -> 104 us
    pallas_call x1, Pallas kernels: 104 us -> 102 us  [local(): pl.pallas_call(kernel, out_shape=shapes, in_specs=[anywhere, anywhere, vm...]
where the time goes in v4:
time: 107 us; the launch traced here: 106 us
  Pallas kernels  104 us (97%)
  between operations  1.29 us (1%)
    pallas_call x1, Pallas kernels, local(): pl.pallas_call(kernel, out_shape=shapes, in_specs=[anywhere, anywhere, vm...  102 us
    pallas_call x1, Pallas kernels, local(): pl.pallas_call(place, out_shape=shapes, in_specs=[anywhere] * 4, out_spec...  2.24 us

profile of v4, /device:TPU:1, one launch (start us, length us, event | category | flops | bytes accessed | tf_op | source)
XLA Modules:
  0.0 105.7 jit_solution(3826315903811379218)
XLA Ops:
  1.3 102.2 %moe_backward.1 = (bf16[64,384]{1,0:T(8,128)(2,1)}, bf16[384,1024]{1,0:T(8,128)(2,1)}, bf16[384,1024]{1,0:T(8,128)(2,1)}, f32[4,384]{1,0:T(4,128)}) custom-call(bf16[64,384]{1,0:T(8,128)(2,1)} %x_hbm.1, bf16[64,384]{1,0:T(8,128)(2,1)} %d_hbm.1, s32[2,64]{1,0:T(2,128)} %bitcast.4, s32[1]{0:T(128)S(6)} %copy.11.live_ref, bf16[4,384]{1,0:T(4,128)(2,1)} %bitcast.3, ...), custom_call_target="tpu_custom_call" | custom-call | tf_op jit(solution)/shard_map/moe_backward/pallas_call | solution.py:611
  103.4 2.2 %place.1 = (bf16[64,384]{1,0:T(8,128)(2,1)}, bf16[384,1024]{1,0:T(8,128)(2,1)}, bf16[384,1024]{1,0:T(8,128)(2,1)}, f32[4,384]{1,0:T(4,128)}) custom-call(bf16[64,384]{1,0:T(8,128)(2,1)} %get-tuple-element.12.refs_0_, bf16[384,1024]{1,0:T(8,128)(2,1)} %get-tuple-element.13.refs_1_, bf16[384,1024]{1,0:T(8,128)(2,1)} %get-tuple-element.14.refs_2_, ...), custom_call_target="tpu_custom_call" | custom-call | tf_op jit(solution)/shard_map/place/pallas_call | solution.py:668
